TPU v7x, 256 devices: a whole 4x4x8 slice. The times are simulated.
256 devices in a mesh: tm: 32 (over y_lo, z, core), blk: 8 (over x, y_hi).
Axes of the slice: x: 4, y: 4 (y_hi: 2, y_lo: 2; y = y_hi * 2 + y_lo), z: 8, core: 2. Of those that a mesh axis runs over, the one named last changes fastest.
Arguments:
- psi_start: float32 [32, 8, 6, 8192], P('tm', 'blk'), may hold values from -6 to 6
- objective: float32 [32, 8, 6, 8192], P('tm', 'blk'), may hold values from -6 to 6
- jacobian: bfloat16 [32, 8, 6, 6, 6, 8192], P('tm', 'blk'), may hold values from -1 to 1
- precond: bfloat16 [32, 8, 6, 6, 8192], P('tm', 'blk'), may hold values from -0.8984375 to 0.8984375
- volume: float32 [8, 8192], P('blk'), may hold values from 0.02 to 0.2
- counts: int32 [8], P('blk'), may hold values from 4096 to 8192, as said below
- neighbours: int32 [8, 6, 8192], P('blk'), may hold values from 0 to 255
- donor: int32 [8, 512], P('blk'), may hold values from 0 to 4095
- match_block: int32 [32, 8, 4], P('tm', 'blk'), may hold values from 0 to 31
- slide: int32 [32, 8, 4], P('tm', 'blk'), may hold values from 0 to 127
Outputs:
- psi: float32 [32, 8, 6, 8192], P('tm', 'blk')
Inputs may be any that keep to these rules, and one draw needn't show every extreme that they name: `counts`: every value lies in 4096 to 8192; some partition holds exactly 8192 live cells.
All inputs are finite; a program needn't handle non-finite values.
Results may differ from a plain program's by a relative error of at most 0.0004.
Values sent between devices are 32-bit elements; how exact they have to be, the bound alone decides.
No kernel may reach another device: no remote copies, remote signals or barrier semaphores. Data moves between devices by JAX's collectives and lax.ppermute only.
A program may use at most 64 MiB of HBM per device.

v0:
```python
import math

import numpy as np
import jax
import jax.numpy as jnp
from jax import lax
from jax.experimental import pallas as pl
from jax.experimental.pallas import tpu as pltpu
from jax.sharding import PartitionSpec as P

SWEEPS = 2
FLUXHINTS = (30000000000, 6000000)
MERGEHINTS = (65536, 65536)
LATE = 1
BIGHINT = 30000000000
F = 6
K = 6
CELLS = 8192
GROUPS = 64
STRIDE = 72
UNROLL = 16
HOPS = (0, 1, 3, 2)
ROWS = F * GROUPS
NT = 32
CHIPS = 16
CHUNK = ROWS // CHIPS
VMEM = pl.BlockSpec(memory_space=pltpu.VMEM)
SMEM = pl.BlockSpec(memory_space=pltpu.SMEM)
ANY = pl.BlockSpec(memory_space=pl.ANY)


def time_kernel():
    n = np.arange(NT)
    parity = np.where(n % 2 == 0, 1.0, -1.0)
    angle = np.where(n == 0, 0.5 * math.pi, math.pi * n / NT)
    sine = np.sin(angle)
    value = 0.5 * parity * np.cos(angle) / sine + 0.125 * parity / (sine * sine)
    return np.where(n == 0, 0.25 * (NT * NT + 2) / 12.0, value).astype(np.float32)


def params(mib=12):
    return pltpu.CompilerParams(vmem_limit_bytes=mib * 1024 * 1024)


def cost(flops, nbytes):
    return pl.CostEstimate(flops=flops, bytes_accessed=nbytes, transcendentals=0)


def f32_rows(n):
    return jax.ShapeDtypeStruct((n, 128), jnp.float32)


def i32_rows(n):
    return jax.ShapeDtypeStruct((n, 128), jnp.int32)


def lane_gather(data, index):
    return jnp.take_along_axis(data, index, axis=1, mode="promise_in_bounds")


def tile(start):
    return pl.ds(pl.multiple_of(start, 8), 8)


def fetch_donor_kernel(psi_hbm, donor_hbm, sent_ref, psi_ref, donor_ref, sems):
    copies = [pltpu.make_async_copy(donor_hbm, donor_ref, sems.at[F])]
    for f in range(F):
        rows = pl.ds(f * GROUPS, GROUPS // 2)
        copies.append(pltpu.make_async_copy(psi_hbm.at[rows, :], psi_ref.at[rows, :], sems.at[f]))
    for copy in copies:
        copy.start()
    for copy in copies:
        copy.wait()
    donor_kernel(psi_ref, donor_ref, sent_ref)


def donor_kernel(psi_ref, donor_ref, sent_ref):
    sublane = lax.broadcasted_iota(jnp.int32, (8, 128), 0)

    def block(q, carry):
        donor = jnp.broadcast_to(donor_ref[pl.ds(q, 1), :], (8, 128))
        lane = donor & 127
        home = (donor >> 7) - sublane
        rows = []
        for f in range(F):
            total = jnp.zeros((8, 128), jnp.float32)
            for b in range(4):
                picked = lane_gather(psi_ref[pl.ds(f * GROUPS + b * 8, 8), :], lane)
                total = total + jnp.where(home == b * 8, picked, 0.0)
            rows.append(jnp.sum(total, axis=0, keepdims=True))
        rows.append(jnp.zeros((2, 128), jnp.float32))
        sent_ref[tile(q * 8), :] = jnp.concatenate(rows, axis=0)
        return carry

    lax.fori_loop(0, 4, block, 0, unroll=2)


def pack_donors(psi, donor):
    return pl.pallas_call(
        fetch_donor_kernel,
        out_shape=f32_rows(32),
        in_specs=[ANY, ANY],
        out_specs=VMEM,
        scratch_shapes=[
            pltpu.VMEM((ROWS, 128), jnp.float32),
            pltpu.VMEM((4, 128), jnp.int32),
            pltpu.SemaphoreType.DMA((F + 1,)),
        ],
        compiler_params=params(50),
        cost_estimate=cost(30000000000, 220000),
        name="pack_donors",
    )(psi, donor)


def merge_kernel(*refs):
    height = refs[0].shape[0]
    for n in range(refs[-1].shape[0] // height):
        refs[-1][pl.ds(n * height, height), :] = refs[n][...]


def merge(hint, pieces, ready=()):
    return pl.pallas_call(
        merge_kernel,
        out_shape=f32_rows(sum(piece.shape[0] for piece in pieces)),
        in_specs=[VMEM] * len(pieces) + [ANY] * len(ready),
        out_specs=VMEM,
        compiler_params=params(),
        cost_estimate=cost(hint, 65536),
        name="merge",
    )(*pieces, *ready)


def prepare_kernel(counts_hbm, pre_hbm, volume_hbm, after_ref, dense_ref, live_ref, scale_ref, pre_ref, volume_ref, counts_ref, sems):
    copies = [
        pltpu.make_async_copy(counts_hbm, counts_ref, sems.at[0]),
        pltpu.make_async_copy(volume_hbm, volume_ref, sems.at[1]),
        pltpu.make_async_copy(pre_hbm, pre_ref, sems.at[2]),
    ]
    for copy in copies:
        copy.start()
    copies[0].wait()
    copies[1].wait()
    for b in range(8):
        live = live_rows(counts_ref, b)
        live_ref[pl.ds(b * 8, 8), :] = live
        scale_ref[pl.ds(b * 8, 8), :] = live * volume_ref[pl.ds(b * 8, 8), :]
    copies[2].wait()

    def step(g, carry):
        at = pl.multiple_of(g * 128, 128)
        for i in range(F):
            dense_ref[pl.ds(i * F * STRIDE + g, F, stride=STRIDE), :] = pre_ref[i, :, pl.ds(at, 128)].astype(jnp.float32)
        return carry

    lax.fori_loop(0, GROUPS, step, 0, unroll=8)


def prepare(counts, precond, volume, after):
    return pl.pallas_call(
        prepare_kernel,
        out_shape=(f32_rows(F * F * STRIDE), f32_rows(GROUPS), f32_rows(GROUPS)),
        in_specs=[ANY] * 4,
        out_specs=(VMEM,) * 3,
        scratch_shapes=[
            pltpu.VMEM((F, F, CELLS), jnp.bfloat16),
            pltpu.VMEM((GROUPS, 128), jnp.float32),
            pltpu.SMEM((1,), jnp.int32),
            pltpu.SemaphoreType.DMA((3,)),
        ],
        compiler_params=params(50),
        cost_estimate=cost(1000000, 2500000),
        name="prepare",
    )(counts, precond, volume, after)


def live_rows(counts_ref, block):
    cell = lax.broadcasted_iota(jnp.int32, (8, 128), 0) * 128 + lax.broadcasted_iota(jnp.int32, (8, 128), 1)
    return jnp.where(cell + block * 1024 < counts_ref[0], 1.0, 0.0)


def flux_kernel(
    counts_hbm, match_hbm, slide_hbm, psi_hbm, nbr_hbm, target_hbm, jac_hbm, *refs
):
    pieces = refs[:-13]
    (out_ref, psi_s, counts_ref, match_ref, slide_ref, nbr_s, target_s, jac_s, stencil_s, pool_s, ghost_s, part_s, sems) = refs[-13:]
    small = [
        pltpu.make_async_copy(counts_hbm, counts_ref, sems.at[8]),
        pltpu.make_async_copy(match_hbm, match_ref, sems.at[9]),
        pltpu.make_async_copy(slide_hbm, slide_ref, sems.at[10]),
    ]
    nbr_copy = pltpu.make_async_copy(nbr_hbm, nbr_s, sems.at[11])
    psi_copy = pltpu.make_async_copy(psi_hbm, psi_s, sems.at[12])
    target_copy = pltpu.make_async_copy(target_hbm, target_s, sems.at[13])

    def jac_copy(b):
        cells = pl.ds(pl.multiple_of(b * 1024, 1024), 1024)
        return pltpu.make_async_copy(jac_hbm.at[:, :, :, cells], jac_s.at[:, :, :, cells], sems.at[b])

    for copy in small:
        copy.start()
    nbr_copy.start()
    psi_copy.start()
    for b in range(8):
        jac_copy(b).start()
    target_copy.start()
    hops = iter(HOPS)
    for piece in pieces:
        for n in range(piece.shape[0] // 64):
            pool_s[pl.ds(next(hops) * 64, 64), :] = piece[pl.ds(n * 64, 64), :]
    stencil_s[...] = jnp.zeros_like(stencil_s)
    own = lax.axis_index("blk")
    lane = lax.broadcasted_iota(jnp.int32, (8, 128), 1)
    for copy in small:
        copy.wait()
    for q in range(4):
        block = match_ref[q]
        part = block // 4
        hop = (part // 2) ^ (own // 2)
        side = lax.rem(part, 2) ^ lax.rem(own, 2)
        source = pool_s[tile((hop * 8 + side * 4 + lax.rem(block, 4)) * 8), :]
        ghost_s[pl.ds(q * 8, 8), :] = lane_gather(source, (lane + slide_ref[q]) & 127)
    nbr_copy.wait()
    for k in range(K):
        for b in range(8):
            stencil_s[pl.ds(b * 64 + k, 8, stride=8), :] = nbr_s[pl.ds(k * GROUPS + b * 8, 8), :]
    psi_copy.wait()
    for b in range(8):
        live = live_rows(counts_ref, b)
        for f in range(F):
            rows = pl.ds(f * GROUPS + b * 8, 8)
            psi_s[rows, :] = psi_s[rows, :] * live

    def step(b, carry):
        for n in range(UNROLL // 8):
            jac_copy(b * (UNROLL // 8) + n).wait()
        for s in range(UNROLL):
            g = b * UNROLL + s
            at = pl.multiple_of(g * 128, 128)
            index = stencil_s[tile(g * 8), :]
            outside = index >= 128
            pick = index & 127
            total = [None] * F
            for j in range(F):
                inner = jnp.broadcast_to(psi_s[pl.ds(j * GROUPS + g, 1), :], (8, 128))
                outer = jnp.broadcast_to(ghost_s[pl.ds((s % 4) * 8 + j, 1), :], (8, 128))
                value = jnp.where(outside, lane_gather(outer, pick), lane_gather(inner, pick))[:K]
                for i in range(F):
                    term = jac_s[i, j, :, pl.ds(at, 128)].astype(jnp.float32) * value
                    total[i] = term if j == 0 else total[i] + term
            for i in range(F):
                part_s[pl.ds(pl.multiple_of(g * 48 + i * 8, 8), K), :] = total[i]
        return carry

    lax.fori_loop(0, GROUPS // UNROLL, step, 0)
    target_copy.wait()

    def gather_up(b, carry):
        for j in range(F):
            flux = part_s[pl.ds(b * 384 + j * 8, 8, stride=48), :]
            for k in range(1, K):
                flux = flux + part_s[pl.ds(b * 384 + j * 8 + k, 8, stride=48), :]
            rows = tile(j * GROUPS + b * 8)
            out_ref[rows, :] = flux - target_s[rows, :]
        return carry

    lax.fori_loop(0, 8, gather_up, 0, unroll=2)


def flux_part(hint, counts, match, slide, psi, neighbours, target, jac, pieces):
    return pl.pallas_call(
        flux_kernel,
        out_shape=(f32_rows(ROWS), f32_rows(ROWS)),
        in_specs=[ANY] * 7 + [VMEM] * len(pieces),
        out_specs=(VMEM, VMEM),
        scratch_shapes=[
            pltpu.SMEM((1,), jnp.int32),
            pltpu.SMEM((4,), jnp.int32),
            pltpu.SMEM((4,), jnp.int32),
            pltpu.VMEM((ROWS, 128), jnp.int32),
            pltpu.VMEM((ROWS, 128), jnp.float32),
            pltpu.VMEM((F, F, K, CELLS), jnp.bfloat16),
            pltpu.VMEM((GROUPS * 8, 128), jnp.int32),
            pltpu.VMEM((256, 128), jnp.float32),
            pltpu.VMEM((32, 128), jnp.float32),
            pltpu.VMEM((GROUPS * 48, 128), jnp.float32),
            pltpu.SemaphoreType.DMA((14,)),
        ],
        compiler_params=params(50),
        cost_estimate=cost(hint, 7000000),
        name="flux_part",
    )(counts, match, slide, psi, neighbours, target, jac, *pieces)


def couple_kernel(own_ref, other_ref, out_hbm, out_ref, sems):
    def put(n):
        rows = pl.ds(n * 8 * CHUNK, 8 * CHUNK)
        return pltpu.make_async_copy(out_ref.at[rows, :], out_hbm.at[rows, :], sems.at[n])

    f = [float(v) for v in time_kernel()]
    first = lax.rem(lax.axis_index("tm"), 2) == 0
    even = f[0::2]
    odd = [jnp.where(first, f[2 * n + 1], f[2 * n - 1]) for n in range(CHIPS)]
    for t0 in range(0, CHIPS, 8):
        for r in range(CHUNK // 8):
            total = [None] * 8
            for s in range(CHIPS):
                own = own_ref[pl.ds(s * CHUNK + r * 8, 8), :]
                other = other_ref[pl.ds(s * CHUNK + r * 8, 8), :]
                for t in range(8):
                    n = (s - t0 - t) % CHIPS
                    term = even[n] * own + odd[n] * other
                    total[t] = term if s == 0 else total[t] + term
            for t in range(8):
                out_ref[pl.ds((t0 + t) * CHUNK + r * 8, 8), :] = total[t]
        put(t0 // 8).start()
    for n in range(2):
        put(n).wait()


def couple(own, other):
    return pl.pallas_call(
        couple_kernel,
        out_shape=f32_rows(ROWS),
        in_specs=[VMEM, VMEM],
        out_specs=ANY,
        scratch_shapes=[pltpu.VMEM((ROWS, 128), jnp.float32), pltpu.SemaphoreType.DMA((2,))],
        compiler_params=params(),
        cost_estimate=cost(3200000, 600000),
        name="couple",
    )(own, other)


def finish_kernel(base_ref, residual_ref, coupling_ref, live_ref, scale_ref, dense_ref, *rest):
    out_hbm = rest[-3] if len(rest) == 3 else rest[1]
    out_ref, sems = rest[-2:]

    def put(half, f):
        rows = pl.ds(f * GROUPS + half * 32, 32)
        return pltpu.make_async_copy(out_ref.at[rows, :], out_hbm.at[rows, :], sems.at[half * F + f])

    def step(b, carry):
        live = live_ref[tile(b * 8), :]
        scale = scale_ref[tile(b * 8), :]
        whole = []
        for j in range(F):
            rows = tile(j * GROUPS + b * 8)
            whole.append(live * residual_ref[rows, :] + scale * coupling_ref[rows, :])
        for i in range(F):
            rows = tile(i * GROUPS + b * 8)
            value = base_ref[rows, :]
            for j in range(F):
                value = value - dense_ref[tile((i * F + j) * STRIDE + b * 8), :] * whole[j]
            out_ref[rows, :] = value
        return carry

    for half in range(2):
        lax.fori_loop(half * 4, half * 4 + 4, step, 0)
        for f in range(F):
            put(half, f).start()
    if len(rest) > 3:
        donor_kernel(out_ref, rest[0], rest[2])
    for half in range(2):
        for f in range(F):
            put(half, f).wait()


def finish(base, residual, coupling, live, scale, dense, donor=None):
    operands = [base, residual, coupling, live, scale, dense] + ([] if donor is None else [donor])
    shapes = [f32_rows(ROWS)] + ([] if donor is None else [f32_rows(32)])
    return pl.pallas_call(
        finish_kernel,
        out_shape=shapes,
        in_specs=[VMEM] * len(operands),
        out_specs=[ANY, VMEM][: len(shapes)],
        scratch_shapes=[pltpu.VMEM((ROWS, 128), jnp.float32), pltpu.SemaphoreType.DMA((2 * F,))],
        compiler_params=params(),
        cost_estimate=cost(600000, 2000000),
        name="finish",
    )(*operands)


def local(
    psi_start, objective, jacobian, precond, volume, counts, neighbours, donor, match_block, slide
):
    by_core = [[2 * chip + core for chip in range(CHIPS)] for core in range(2)]
    swap_core = [(i, i ^ 1) for i in range(NT)]

    def across(x):
        moved = lax.all_to_all(x.reshape(CHIPS, CHUNK, 128), "tm", 0, 0, axis_index_groups=by_core)
        return moved.reshape(ROWS, 128)
    def blk_swap(x, bits):
        return lax.ppermute(x, "blk", [(i, i ^ bits) for i in range(8)])

    psi = psi_start.reshape(ROWS, 128)
    target = objective.reshape(ROWS, 128)
    faces = donor.reshape(4, 128)
    nearby = neighbours.reshape(ROWS, 128)
    match, slides = match_block.reshape(4), slide.reshape(4)
    sent = pack_donors(psi, faces)
    for sweep in range(SWEEPS):
        both = merge(MERGEHINTS[sweep], [sent, blk_swap(sent, 1)], [counts] if sweep == 0 else [])
        pieces = [both] + [blk_swap(both, 2 * hop) for hop in HOPS[1:]]
        if sweep == 0:
            psi, sent = lax.optimization_barrier((psi, sent))
        states = across(psi)
        states, pieces[0] = lax.optimization_barrier((states, pieces[0]))
        coupling = across(couple(states, lax.ppermute(states, "tm", swap_core)))
        if sweep == LATE:
            pieces = [merge(BIGHINT, pieces[:3]), pieces[3]]
        residual, base = flux_part(FLUXHINTS[sweep], counts, match, slides, psi, nearby, target, jacobian[0, 0], pieces)
        if sweep == 0:
            dense, live, scale = prepare(counts, precond[0, 0], volume.reshape(GROUPS, 128), residual)
        more = [faces] if sweep + 1 < SWEEPS else []
        psi, *rest = finish(base, residual, coupling, live, scale, dense, *more)
        if rest:
            sent = rest[0]
    return psi.reshape(1, 1, F, CELLS)


def solution(mesh):
    in_specs = (
        P("tm", "blk", None, None),
        P("tm", "blk", None, None),
        P("tm", "blk", None, None, None, None),
        P("tm", "blk", None, None, None),
        P("blk", None),
        P("blk"),
        P("blk", None, None),
        P("blk", None),
        P("tm", "blk", None),
        P("tm", "blk", None),
    )
    out_specs = P("tm", "blk", None, None)
    return jax.shard_map(local, mesh=mesh, in_specs=in_specs, out_specs=out_specs, check_vma=False)
```

profile of v0, /device:TPU:32, one launch (start us, length us, event | category | flops | bytes accessed | tf_op | source)
XLA Modules:
  0.0 73.7 jit_solution(1023530151807393177)
XLA Ops:
  0.0 0.0 copy-start.4
  0.0 0.7 copy-done.4
  0.7 0.0 copy-start.1
  0.7 0.0 copy-start.2
  0.7 0.0 copy-start.6
  0.7 0.0 copy-start.7
  0.7 1.2 %pack_donors.1.refs_0_ = f32[32,128]{1,0:T(8,128)S(1)} custom-call(f32[384,128]{1,0:T(8,128)} %bitcast.2.psi_hbm, s32[4,128]{1,0:T(4,128)S(1)} %bitcast.30), custom_call_target="tpu_custom_call" | custom-call | flops 30000001024 | bytes 220000 | tf_op jit(solution)/shard_map/pack_donors/pallas_call | solution.py:99
  1.9 9.6 %all-to-all-start = ((f32[16,24,128]{2,1,0:T(8,128)}), f32[16,24,128]{2,1,0:T(8,128)S(1)}, u32[]{:S(2)}, u32[]{:S(2)}) async-start(f32[16,24,128]{2,1,0:T(8,128)} %bitcast.7), calls=%async_computation | async-start | bytes 393216 | tf_op jit(solution)/shard_map/all_to_all | solution.py:389
  11.5 2.9 %collective-permute-start = (f32[32,128]{1,0:T(8,128)S(1)}, f32[32,128]{1,0:T(8,128)S(1)}, u32[]{:S(2)}, u32[]{:S(2)}) collective-permute-start(f32[32,128]{1,0:T(8,128)S(1)} %pack_donors.1.refs_0_), channel_id=1, source_target_pairs={{0,1},{1,0},{2,3},{3,2},{4,5},{5,4},{6,7},{7,6},{8,9},{9,8},{10,11... | collective-permute-start | bytes 49160 | tf_op jit(solution)/shard_map/ppermute | solution.py:392
  15.0 1.8 %collective-permute-done.refs_1_ = f32[32,128]{1,0:T(8,128)S(1)} collective-permute-done((f32[32,128]{1,0:T(8,128)S(1)}, f32[32,128]{1,0:T(8,128)S(1)}, u32[]{:S(2)}, u32[]{:S(2)}) %collective-permute-start) | collective-permute-done | bytes 16416 | tf_op jit(solution)/shard_map/ppermute | solution.py:392
  16.9 3.8 %all-to-all-done = f32[16,24,128]{2,1,0:T(8,128)S(1)} async-done(((f32[16,24,128]{2,1,0:T(8,128)}), f32[16,24,128]{2,1,0:T(8,128)S(1)}, u32[]{:S(2)}, u32[]{:S(2)}) %all-to-all-start) | async-done | bytes 196640 | tf_op jit(solution)/shard_map/all_to_all | solution.py:389
  20.7 0.0 collective-permute-start.4
  20.7 3.0 %collective-permute-start.3 = (f32[64,128]{1,0:T(8,128)S(1)}, f32[64,128]{1,0:T(8,128)S(1)}, u32[]{:S(2)}, u32[]{:S(2)}) collective-permute-start(f32[64,128]{1,0:T(8,128)S(1)} %merge.3.refs_0_), channel_id=1, source_target_pairs={{0,4},{1,5},{2,6},{3,7},{4,0},{5,1},{6,2},{7,3},{8,12},{9,13},{10,... | collective-permute-start | bytes 98312 | tf_op jit(solution)/shard_map/ppermute | solution.py:392
  23.7 1.1 %collective-permute-start.2 = (f32[64,128]{1,0:T(8,128)S(1)}, f32[64,128]{1,0:T(8,128)S(1)}, u32[]{:S(2)}, u32[]{:S(2)}) collective-permute-start(f32[64,128]{1,0:T(8,128)S(1)} %merge.3.refs_0_), channel_id=1, source_target_pairs={{0,6},{1,7},{2,4},{3,5},{4,2},{5,3},{6,0},{7,1},{8,14},{9,15},{10,... | collective-permute-start | bytes 98312 | tf_op jit(solution)/shard_map/ppermute | solution.py:392
  24.9 0.0 collective-permute-start.1
  24.9 0.0 collective-permute-done.4.other_ref
  24.9 1.1 %couple.2 = f32[384,128]{1,0:T(8,128)} custom-call(f32[384,128]{1,0:T(8,128)S(1)} %bitcast.22, f32[384,128]{1,0:T(8,128)S(1)} %collective-permute-done.4.other_ref), custom_call_target="tpu_custom_call" | custom-call | flops 3200000 | bytes 600000 | tf_op jit(solution)/shard_map/couple/pallas_call | solution.py:321
  25.9 4.3 %all-to-all-start.1 = ((f32[16,24,128]{2,1,0:T(8,128)}), f32[16,24,128]{2,1,0:T(8,128)S(1)}, u32[]{:S(2)}, u32[]{:S(2)}) async-start(f32[16,24,128]{2,1,0:T(8,128)} %bitcast.9), calls=%async_computation.1 | async-start | bytes 393216 | tf_op jit(solution)/shard_map/all_to_all | solution.py:389
  30.3 0.0 collective-permute-done.3.refs_3_
  30.3 0.0 collective-permute-done.2.refs_2_
  30.3 0.0 collective-permute-done.1.refs_1_
  30.3 0.0 copy-done.1
  30.3 0.0 copy-done.2
  30.3 0.0 copy-done.6
  30.3 0.0 copy-done.7
  30.4 0.0 copy-start
  30.4 0.0 copy-start.3
  30.4 0.0 copy-start.5
  30.4 3.7 %flux_part.2 = (f32[384,128]{1,0:T(8,128)S(1)}, f32[384,128]{1,0:T(8,128)S(1)}) custom-call(s32[1]{0:T(128)S(6)} %copy.13.refs_2_.counts_hbm, s32[4]{0:T(128)S(1)} %bitcast.32, s32[4]{0:T(128)S(1)} %bitcast.34, f32[384,128]{1,0:T(8,128)} %bitcast.2.psi_hbm, s32[384,128]{1,0:T(8,128)S(1)} %bitcast.25, f32[384,128]{1,0:T(8,128)S(1)} %bitcast.27, ...), custom_call_target="tpu_custom_call" | custom-call | flops 30000001024 | bytes 7000000 | tf_op jit(solution)/shard_map/flux_part/pallas_call | solution.py:270
  34.1 0.0 copy-done
  34.1 0.0 copy-done.3
  34.1 0.9 %prepare.1 = (f32[2592,128]{1,0:T(8,128)S(1)}, f32[64,128]{1,0:T(8,128)S(1)}, f32[64,128]{1,0:T(8,128)S(1)}) custom-call(s32[1]{0:T(128)S(6)} %copy.13.refs_2_.counts_hbm, bf16[6,6,8192]{2,1,0:T(8,128)(2,1)S(1)} %bitcast.20, f32[64,128]{1,0:T(8,128)S(1)} %bitcast.29, f32[384,128]{1,0:T(8,128)S(1)} %get-tuple-element.22.after_ref.residual_ref), custom_call_target="tpu_custom_call" | custom-call | flops 1000000 | bytes 2500000 | tf_op jit(solution)/shard_map/prepare/pallas_call | solution.py:159
  35.0 4.5 %all-to-all-done.1 = f32[16,24,128]{2,1,0:T(8,128)S(1)} async-done(((f32[16,24,128]{2,1,0:T(8,128)}), f32[16,24,128]{2,1,0:T(8,128)S(1)}, u32[]{:S(2)}, u32[]{:S(2)}) %all-to-all-start.1) | async-done | bytes 196640 | tf_op jit(solution)/shard_map/all_to_all | solution.py:389
  39.5 0.0 copy-done.5
  39.5 0.9 %finish.2 = (f32[384,128]{1,0:T(8,128)}, f32[32,128]{1,0:T(8,128)S(1)}) custom-call(f32[384,128]{1,0:T(8,128)S(1)} %get-tuple-element.21.base_ref, f32[384,128]{1,0:T(8,128)S(1)} %get-tuple-element.22.after_ref.residual_ref, f32[384,128]{1,0:T(8,128)S(1)} %bitcast.18, f32[64,128]{1,0:T(8,128)S(1)} %get-tuple-element.24.live_ref, ...), custom_call_target="tpu_custom_call" | custom-call | flops 600000 | bytes 2000000 | tf_op jit(solution)/shard_map/finish/pallas_call | solution.py:370
  40.5 4.0 %all-to-all-start.2 = ((f32[16,24,128]{2,1,0:T(8,128)}), f32[16,24,128]{2,1,0:T(8,128)S(1)}, u32[]{:S(2)}, u32[]{:S(2)}) async-start(f32[16,24,128]{2,1,0:T(8,128)} %bitcast.13), calls=%async_computation.2 | async-start | bytes 393216 | tf_op jit(solution)/shard_map/all_to_all | solution.py:389
  44.5 3.1 %collective-permute-start.5 = (f32[32,128]{1,0:T(8,128)S(1)}, f32[32,128]{1,0:T(8,128)S(1)}, u32[]{:S(2)}, u32[]{:S(2)}) collective-permute-start(f32[32,128]{1,0:T(8,128)S(1)} %get-tuple-element.28.refs_0_), channel_id=1, source_target_pairs={{0,1},{1,0},{2,3},{3,2},{4,5},{5,4},{6,7},{7,6},{8,9},{9,8},{10,11... | collective-permute-start | bytes 49160 | tf_op jit(solution)/shard_map/ppermute | solution.py:392
  47.6 2.3 %collective-permute-done.5.refs_1_ = f32[32,128]{1,0:T(8,128)S(1)} collective-permute-done((f32[32,128]{1,0:T(8,128)S(1)}, f32[32,128]{1,0:T(8,128)S(1)}, u32[]{:S(2)}, u32[]{:S(2)}) %collective-permute-start.5) | collective-permute-done | bytes 16416 | tf_op jit(solution)/shard_map/ppermute | solution.py:392
  50.0 3.3 %all-to-all-done.2 = f32[16,24,128]{2,1,0:T(8,128)S(1)} async-done(((f32[16,24,128]{2,1,0:T(8,128)}), f32[16,24,128]{2,1,0:T(8,128)S(1)}, u32[]{:S(2)}, u32[]{:S(2)}) %all-to-all-start.2) | async-done | bytes 196640 | tf_op jit(solution)/shard_map/all_to_all | solution.py:389
  53.2 0.0 collective-permute-start.9
  53.2 2.1 %collective-permute-start.7 = (f32[64,128]{1,0:T(8,128)S(1)}, f32[64,128]{1,0:T(8,128)S(1)}, u32[]{:S(2)}, u32[]{:S(2)}) collective-permute-start(f32[64,128]{1,0:T(8,128)S(1)} %merge.4.refs_0_), channel_id=1, source_target_pairs={{0,6},{1,7},{2,4},{3,5},{4,2},{5,3},{6,0},{7,1},{8,14},{9,15},{10,... | collective-permute-start | bytes 98312 | tf_op jit(solution)/shard_map/ppermute | solution.py:392
  55.3 0.9 %collective-permute-start.6 = (f32[64,128]{1,0:T(8,128)S(1)}, f32[64,128]{1,0:T(8,128)S(1)}, u32[]{:S(2)}, u32[]{:S(2)}) collective-permute-start(f32[64,128]{1,0:T(8,128)S(1)} %merge.4.refs_0_), channel_id=1, source_target_pairs={{0,2},{1,3},{2,0},{3,1},{4,6},{5,7},{6,4},{7,5},{8,10},{9,11},{10,... | collective-permute-start | bytes 98312 | tf_op jit(solution)/shard_map/ppermute | solution.py:392
  56.2 1.7 %collective-permute-start.8 = (f32[64,128]{1,0:T(8,128)S(1)}, f32[64,128]{1,0:T(8,128)S(1)}, u32[]{:S(2)}, u32[]{:S(2)}) collective-permute-start(f32[64,128]{1,0:T(8,128)S(1)} %merge.4.refs_0_), channel_id=1, source_target_pairs={{0,4},{1,5},{2,6},{3,7},{4,0},{5,1},{6,2},{7,3},{8,12},{9,13},{10,... | collective-permute-start | bytes 98312 | tf_op jit(solution)/shard_map/ppermute | solution.py:392
  57.9 0.0 collective-permute-done.9.other_ref
  57.9 1.1 %couple.3 = f32[384,128]{1,0:T(8,128)} custom-call(f32[384,128]{1,0:T(8,128)S(1)} %bitcast.24, f32[384,128]{1,0:T(8,128)S(1)} %collective-permute-done.9.other_ref), custom_call_target="tpu_custom_call" | custom-call | flops 3200000 | bytes 600000 | tf_op jit(solution)/shard_map/couple/pallas_call | solution.py:321
  59.0 4.9 %all-to-all-start.3 = ((f32[16,24,128]{2,1,0:T(8,128)}), f32[16,24,128]{2,1,0:T(8,128)S(1)}, u32[]{:S(2)}, u32[]{:S(2)}) async-start(f32[16,24,128]{2,1,0:T(8,128)} %bitcast.15), calls=%async_computation.3 | async-start | bytes 393216 | tf_op jit(solution)/shard_map/all_to_all | solution.py:389
  63.9 0.0 collective-permute-done.7.refs_2_
  63.9 0.0 collective-permute-done.6.refs_1_
  63.9 0.0 collective-permute-done.8.refs_1_
  63.9 3.7 %flux_part.3 = (f32[384,128]{1,0:T(8,128)S(1)}, f32[384,128]{1,0:T(8,128)S(1)}) custom-call(s32[1]{0:T(128)S(6)} %copy.13.refs_2_.counts_hbm, s32[4]{0:T(128)S(1)} %bitcast.33, s32[4]{0:T(128)S(1)} %bitcast.35, f32[384,128]{1,0:T(8,128)} %get-tuple-element.27.psi_hbm, s32[384,128]{1,0:T(8,128)S(1)} %bitcast.26, f32[384,128]{1,0:T(8,128)S(1)} %bitcast.28, ...), custom_call_target="tpu_custom_call" | custom-call | flops 6000000 | bytes 7000000 | tf_op jit(solution)/shard_map/flux_part/pallas_call | solution.py:270
  67.6 5.2 %all-to-all-done.3 = f32[16,24,128]{2,1,0:T(8,128)S(1)} async-done(((f32[16,24,128]{2,1,0:T(8,128)}), f32[16,24,128]{2,1,0:T(8,128)S(1)}, u32[]{:S(2)}, u32[]{:S(2)}) %all-to-all-start.3) | async-done | bytes 196640 | tf_op jit(solution)/shard_map/all_to_all | solution.py:389
  72.8 0.9 %finish.3 = f32[384,128]{1,0:T(8,128)} custom-call(f32[384,128]{1,0:T(8,128)S(1)} %get-tuple-element.30.base_ref, f32[384,128]{1,0:T(8,128)S(1)} %get-tuple-element.31.residual_ref, f32[384,128]{1,0:T(8,128)S(1)} %bitcast.19, f32[64,128]{1,0:T(8,128)S(1)} %get-tuple-element.24.live_ref, f32[64,128]{1,0:T(8,128)S(1)} %get-tuple-element.25.scale_ref, ...), custom_call_target="tpu_custom_call" | custom-call | flops 600000 | bytes 2000000 | tf_op jit(solution)/shard_map/finish/pallas_call | solution.py:370
  (3 shorter events, 0.0 us)
Async XLA Ops:
  0.0 0.7 copy-start.4
  0.7 29.6 %copy-start.1 = (s32[1,6,8192]{2,0,1:T(1,128)S(1)}, s32[1,6,8192]{2,0,1:T(1,128)}, u32[]{:S(2)}) copy-start(s32[1,6,8192]{2,0,1:T(1,128)} %param.16) | copy-start | bytes 589828
  0.7 29.6 %copy-start.2 = (f32[1,1,6,8192]{3,1,2,0:T(1,128)S(1)}, f32[1,1,6,8192]{3,1,2,0:T(1,128)}, u32[]{:S(2)}) copy-start(f32[1,1,6,8192]{3,1,2,0:T(1,128)} %param.11) | copy-start | bytes 589828
  0.7 29.7 %copy-start.6 = (s32[1,1,4]{2,1,0:T(1,128)S(1)}, s32[1,1,4]{2,1,0:T(1,128)}, u32[]{:S(2)}) copy-start(s32[1,1,4]{2,1,0:T(1,128)} %param.18) | copy-start | bytes 52
  0.7 29.7 %copy-start.7 = (s32[1,1,4]{2,1,0:T(1,128)S(1)}, s32[1,1,4]{2,1,0:T(1,128)}, u32[]{:S(2)}) copy-start(s32[1,1,4]{2,1,0:T(1,128)} %param.19) | copy-start | bytes 52
  1.9 18.8 %all-to-all-start = ((f32[16,24,128]{2,1,0:T(8,128)}), f32[16,24,128]{2,1,0:T(8,128)S(1)}, u32[]{:S(2)}, u32[]{:S(2)}) async-start(f32[16,24,128]{2,1,0:T(8,128)} %bitcast.7), calls=%async_computation | async-start | bytes 393216 | tf_op jit(solution)/shard_map/all_to_all | solution.py:389
  11.5 5.4 %collective-permute-start = (f32[32,128]{1,0:T(8,128)S(1)}, f32[32,128]{1,0:T(8,128)S(1)}, u32[]{:S(2)}, u32[]{:S(2)}) collective-permute-start(f32[32,128]{1,0:T(8,128)S(1)} %pack_donors.1.refs_0_), channel_id=1, source_target_pairs={{0,1},{1,0},{2,3},{3,2},{4,5},{5,4},{6,7},{7,6},{8,9},{9,8},{10,11... | collective-permute-start | bytes 49160 | tf_op jit(solution)/shard_map/ppermute | solution.py:392
  20.7 4.2 %collective-permute-start.4 = (f32[384,128]{1,0:T(8,128)S(1)}, f32[384,128]{1,0:T(8,128)S(1)}, u32[]{:S(2)}, u32[]{:S(2)}) collective-permute-start(f32[384,128]{1,0:T(8,128)S(1)} %bitcast.21), channel_id=1, source_target_pairs={{0,8},{8,0},{16,24},{24,16},{32,40},{40,32},{48,56},{56,48},{64,72... | collective-permute-start | bytes 589832 | tf_op jit(solution)/shard_map/ppermute | solution.py:407
  20.7 9.6 %collective-permute-start.3 = (f32[64,128]{1,0:T(8,128)S(1)}, f32[64,128]{1,0:T(8,128)S(1)}, u32[]{:S(2)}, u32[]{:S(2)}) collective-permute-start(f32[64,128]{1,0:T(8,128)S(1)} %merge.3.refs_0_), channel_id=1, source_target_pairs={{0,4},{1,5},{2,6},{3,7},{4,0},{5,1},{6,2},{7,3},{8,12},{9,13},{10,... | collective-permute-start | bytes 98312 | tf_op jit(solution)/shard_map/ppermute | solution.py:392
  23.7 6.6 %collective-permute-start.2 = (f32[64,128]{1,0:T(8,128)S(1)}, f32[64,128]{1,0:T(8,128)S(1)}, u32[]{:S(2)}, u32[]{:S(2)}) collective-permute-start(f32[64,128]{1,0:T(8,128)S(1)} %merge.3.refs_0_), channel_id=1, source_target_pairs={{0,6},{1,7},{2,4},{3,5},{4,2},{5,3},{6,0},{7,1},{8,14},{9,15},{10,... | collective-permute-start | bytes 98312 | tf_op jit(solution)/shard_map/ppermute | solution.py:392
  24.9 5.5 %collective-permute-start.1 = (f32[64,128]{1,0:T(8,128)S(1)}, f32[64,128]{1,0:T(8,128)S(1)}, u32[]{:S(2)}, u32[]{:S(2)}) collective-permute-start(f32[64,128]{1,0:T(8,128)S(1)} %merge.3.refs_0_), channel_id=1, source_target_pairs={{0,2},{1,3},{2,0},{3,1},{4,6},{5,7},{6,4},{7,5},{8,10},{9,11},{10,... | collective-permute-start | bytes 98312 | tf_op jit(solution)/shard_map/ppermute | solution.py:392
  25.9 13.6 %all-to-all-start.1 = ((f32[16,24,128]{2,1,0:T(8,128)}), f32[16,24,128]{2,1,0:T(8,128)S(1)}, u32[]{:S(2)}, u32[]{:S(2)}) async-start(f32[16,24,128]{2,1,0:T(8,128)} %bitcast.9), calls=%async_computation.1 | async-start | bytes 393216 | tf_op jit(solution)/shard_map/all_to_all | solution.py:389
  30.4 3.7 %copy-start = (bf16[1,1,6,6,8192]{4,3,2,1,0:T(8,128)(2,1)S(1)}, bf16[1,1,6,6,8192]{4,3,2,1,0:T(8,128)(2,1)}, u32[]{:S(2)}) copy-start(bf16[1,1,6,6,8192]{4,3,2,1,0:T(8,128)(2,1)} %param.13) | copy-start | bytes 1769476
  30.4 3.7 %copy-start.3 = (f32[1,8192]{1,0:T(1,128)S(1)}, f32[1,8192]{1,0:T(1,128)}, u32[]{:S(2)}) copy-start(f32[1,8192]{1,0:T(1,128)} %param.14) | copy-start | bytes 98308
  30.4 9.2 %copy-start.5 = (s32[1,512]{1,0:T(1,128)S(1)}, s32[1,512]{1,0:T(1,128)}, u32[]{:S(2)}) copy-start(s32[1,512]{1,0:T(1,128)} %param.17) | copy-start | bytes 6148
  40.5 12.8 %all-to-all-start.2 = ((f32[16,24,128]{2,1,0:T(8,128)}), f32[16,24,128]{2,1,0:T(8,128)S(1)}, u32[]{:S(2)}, u32[]{:S(2)}) async-start(f32[16,24,128]{2,1,0:T(8,128)} %bitcast.13), calls=%async_computation.2 | async-start | bytes 393216 | tf_op jit(solution)/shard_map/all_to_all | solution.py:389
  44.5 5.5 %collective-permute-start.5 = (f32[32,128]{1,0:T(8,128)S(1)}, f32[32,128]{1,0:T(8,128)S(1)}, u32[]{:S(2)}, u32[]{:S(2)}) collective-permute-start(f32[32,128]{1,0:T(8,128)S(1)} %get-tuple-element.28.refs_0_), channel_id=1, source_target_pairs={{0,1},{1,0},{2,3},{3,2},{4,5},{5,4},{6,7},{7,6},{8,9},{9,8},{10,11... | collective-permute-start | bytes 49160 | tf_op jit(solution)/shard_map/ppermute | solution.py:392
  53.2 4.7 %collective-permute-start.9 = (f32[384,128]{1,0:T(8,128)S(1)}, f32[384,128]{1,0:T(8,128)S(1)}, u32[]{:S(2)}, u32[]{:S(2)}) collective-permute-start(f32[384,128]{1,0:T(8,128)S(1)} %bitcast.23), channel_id=1, source_target_pairs={{0,8},{8,0},{16,24},{24,16},{32,40},{40,32},{48,56},{56,48},{64,72... | collective-permute-start | bytes 589832 | tf_op jit(solution)/shard_map/ppermute | solution.py:407
  53.2 10.7 %collective-permute-start.7 = (f32[64,128]{1,0:T(8,128)S(1)}, f32[64,128]{1,0:T(8,128)S(1)}, u32[]{:S(2)}, u32[]{:S(2)}) collective-permute-start(f32[64,128]{1,0:T(8,128)S(1)} %merge.4.refs_0_), channel_id=1, source_target_pairs={{0,6},{1,7},{2,4},{3,5},{4,2},{5,3},{6,0},{7,1},{8,14},{9,15},{10,... | collective-permute-start | bytes 98312 | tf_op jit(solution)/shard_map/ppermute | solution.py:392
  55.3 8.6 %collective-permute-start.6 = (f32[64,128]{1,0:T(8,128)S(1)}, f32[64,128]{1,0:T(8,128)S(1)}, u32[]{:S(2)}, u32[]{:S(2)}) collective-permute-start(f32[64,128]{1,0:T(8,128)S(1)} %merge.4.refs_0_), channel_id=1, source_target_pairs={{0,2},{1,3},{2,0},{3,1},{4,6},{5,7},{6,4},{7,5},{8,10},{9,11},{10,... | collective-permute-start | bytes 98312 | tf_op jit(solution)/shard_map/ppermute | solution.py:392
  56.2 7.7 %collective-permute-start.8 = (f32[64,128]{1,0:T(8,128)S(1)}, f32[64,128]{1,0:T(8,128)S(1)}, u32[]{:S(2)}, u32[]{:S(2)}) collective-permute-start(f32[64,128]{1,0:T(8,128)S(1)} %merge.4.refs_0_), channel_id=1, source_target_pairs={{0,4},{1,5},{2,6},{3,7},{4,0},{5,1},{6,2},{7,3},{8,12},{9,13},{10,... | collective-permute-start | bytes 98312 | tf_op jit(solution)/shard_map/ppermute | solution.py:392
  59.0 13.8 %all-to-all-start.3 = ((f32[16,24,128]{2,1,0:T(8,128)}), f32[16,24,128]{2,1,0:T(8,128)S(1)}, u32[]{:S(2)}, u32[]{:S(2)}) async-start(f32[16,24,128]{2,1,0:T(8,128)} %bitcast.15), calls=%async_computation.3 | async-start | bytes 393216 | tf_op jit(solution)/shard_map/all_to_all | solution.py:389
where the time goes:
time: 74.4 us; the launch traced here: 73.7 us
  starting transfers between devices  37.8 us (51%)
  waiting for transfers between devices  21 us (28%)
  Pallas kernels  13.4 us (18%)
  between operations  0.84 us (1%)
    all_to_all x4, starting transfers between devices, across(): lax.all_to_all(x.reshape(CHIPS, CHUNK, 128), 'tm', 0, 0, axis_index_group...  22.9 us
    all_to_all x4, waiting for transfers between devices, across(): lax.all_to_all(x.reshape(CHIPS, CHUNK, 128), 'tm', 0, 0, axis_index_group...  16.8 us
    ppermute x8, starting transfers between devices, blk_swap(): return lax.ppermute(x, 'blk', [(i, i ^ bits) for i in range(8)])  14.9 us
    pallas_call x2, Pallas kernels, flux_part(): pl.pallas_call(flux_kernel, out_shape=(f32_rows(ROWS), f32_rows(ROWS)), i...  7.31 us
    ppermute x8, waiting for transfers between devices, blk_swap(): return lax.ppermute(x, 'blk', [(i, i ^ bits) for i in range(8)])  4.15 us
    pallas_call x2, Pallas kernels, couple(): pl.pallas_call(couple_kernel, out_shape=f32_rows(ROWS), in_specs=[VMEM, V...  2.15 us
    pallas_call x2, Pallas kernels, finish(): pl.pallas_call(finish_kernel, out_shape=shapes, in_specs=[VMEM] * len(ope...  1.84 us
  transfers between devices with their start and end apart: 14, of which 6 were waited for; matrix products, arithmetic and copies ran while one was open for 0% of the time, Pallas kernels for 14%

commit v1 on v0

--- a/solution.py
+++ b/solution.py
@@ -9,17 +9,15 @@
 from jax.sharding import PartitionSpec as P
 
 SWEEPS = 2
-FLUXHINTS = (30000000000, 6000000)
+FLUXHINTS = (30000000000, 30000000000)
 MERGEHINTS = (65536, 65536)
-LATE = 1
-BIGHINT = 30000000000
 F = 6
 K = 6
 CELLS = 8192
 GROUPS = 64
 STRIDE = 72
 UNROLL = 16
-HOPS = (0, 1, 3, 2)
+HOPS = (0, 1, 2, 3)
 ROWS = F * GROUPS
 NT = 32
 CHIPS = 16
@@ -405,8 +403,6 @@
         states = across(psi)
         states, pieces[0] = lax.optimization_barrier((states, pieces[0]))
         coupling = across(couple(states, lax.ppermute(states, "tm", swap_core)))
-        if sweep == LATE:
-            pieces = [merge(BIGHINT, pieces[:3]), pieces[3]]
         residual, base = flux_part(FLUXHINTS[sweep], counts, match, slides, psi, nearby, target, jacobian[0, 0], pieces)
         if sweep == 0:
             dense, live, scale = prepare(counts, precond[0, 0], volume.reshape(GROUPS, 128), residual)

time: 74.4 us -> 73.5 us (0.988)
  no operation moved by 1% of the time
where the time goes in v1:
time: 73.5 us; the launch traced here: 72.8 us
  starting transfers between devices  37.4 us (51%)
  waiting for transfers between devices  20.4 us (28%)
  Pallas kernels  13.4 us (18%)
  between operations  0.84 us (1%)
    all_to_all x4, starting transfers between devices, across(): lax.all_to_all(x.reshape(CHIPS, CHUNK, 128), 'tm', 0, 0, axis_index_group...  23.2 us
    all_to_all x4, waiting for transfers between devices, across(): lax.all_to_all(x.reshape(CHIPS, CHUNK, 128), 'tm', 0, 0, axis_index_group...  16.4 us
    ppermute x8, starting transfers between devices, blk_swap(): return lax.ppermute(x, 'blk', [(i, i ^ bits) for i in range(8)])  14.2 us
    pallas_call x2, Pallas kernels, flux_part(): pl.pallas_call(flux_kernel, out_shape=(f32_rows(ROWS), f32_rows(ROWS)), i...  7.31 us
    ppermute x8, waiting for transfers between devices, blk_swap(): return lax.ppermute(x, 'blk', [(i, i ^ bits) for i in range(8)])  3.97 us
    pallas_call x2, Pallas kernels, couple(): pl.pallas_call(couple_kernel, out_shape=f32_rows(ROWS), in_specs=[VMEM, V...  2.14 us
    pallas_call x2, Pallas kernels, finish(): pl.pallas_call(finish_kernel, out_shape=shapes, in_specs=[VMEM] * len(ope...  1.84 us
  transfers between devices with their start and end apart: 14, of which 6 were waited for; matrix products, arithmetic and copies ran while one was open for 0% of the time, Pallas kernels for 14%

profile of v1, /device:TPU:32, one launch (start us, length us, event | category | flops | bytes accessed | tf_op | source)
XLA Modules:
  0.0 72.8 jit_solution(9915341706920847829)
XLA Ops:
  0.0 0.0 copy-start.2
  0.0 0.7 copy-done.2
  0.7 0.0 copy-start.4
  0.7 0.0 copy-start.5
  0.7 0.0 copy-start.6
  0.7 0.0 copy-start.7
  0.7 1.2 %pack_donors.1.refs_0_ = f32[32,128]{1,0:T(8,128)S(1)} custom-call(f32[384,128]{1,0:T(8,128)} %bitcast.2.psi_hbm, s32[4,128]{1,0:T(4,128)S(1)} %bitcast.26), custom_call_target="tpu_custom_call" | custom-call | flops 30000001024 | bytes 220000 | tf_op jit(solution)/shard_map/pack_donors/pallas_call | solution.py:97
  1.9 9.6 %all-to-all-start = ((f32[16,24,128]{2,1,0:T(8,128)}), f32[16,24,128]{2,1,0:T(8,128)S(1)}, u32[]{:S(2)}, u32[]{:S(2)}) async-start(f32[16,24,128]{2,1,0:T(8,128)} %bitcast.7), calls=%async_computation | async-start | bytes 393216 | tf_op jit(solution)/shard_map/all_to_all | solution.py:387
  11.5 2.9 %collective-permute-start = (f32[32,128]{1,0:T(8,128)S(1)}, f32[32,128]{1,0:T(8,128)S(1)}, u32[]{:S(2)}, u32[]{:S(2)}) collective-permute-start(f32[32,128]{1,0:T(8,128)S(1)} %pack_donors.1.refs_0_), channel_id=1, source_target_pairs={{0,1},{1,0},{2,3},{3,2},{4,5},{5,4},{6,7},{7,6},{8,9},{9,8},{10,11... | collective-permute-start | bytes 49160 | tf_op jit(solution)/shard_map/ppermute | solution.py:390
  15.0 1.8 %collective-permute-done.refs_1_ = f32[32,128]{1,0:T(8,128)S(1)} collective-permute-done((f32[32,128]{1,0:T(8,128)S(1)}, f32[32,128]{1,0:T(8,128)S(1)}, u32[]{:S(2)}, u32[]{:S(2)}) %collective-permute-start) | collective-permute-done | bytes 16416 | tf_op jit(solution)/shard_map/ppermute | solution.py:390
  16.9 3.8 %all-to-all-done = f32[16,24,128]{2,1,0:T(8,128)S(1)} async-done(((f32[16,24,128]{2,1,0:T(8,128)}), f32[16,24,128]{2,1,0:T(8,128)S(1)}, u32[]{:S(2)}, u32[]{:S(2)}) %all-to-all-start) | async-done | bytes 196640 | tf_op jit(solution)/shard_map/all_to_all | solution.py:387
  20.7 0.0 collective-permute-start.4
  20.7 2.8 %collective-permute-start.3 = (f32[64,128]{1,0:T(8,128)S(1)}, f32[64,128]{1,0:T(8,128)S(1)}, u32[]{:S(2)}, u32[]{:S(2)}) collective-permute-start(f32[64,128]{1,0:T(8,128)S(1)} %merge.2.refs_0_), channel_id=1, source_target_pairs={{0,6},{1,7},{2,4},{3,5},{4,2},{5,3},{6,0},{7,1},{8,14},{9,15},{10,... | collective-permute-start | bytes 98312 | tf_op jit(solution)/shard_map/ppermute | solution.py:390
  23.4 0.8 %collective-permute-start.2 = (f32[64,128]{1,0:T(8,128)S(1)}, f32[64,128]{1,0:T(8,128)S(1)}, u32[]{:S(2)}, u32[]{:S(2)}) collective-permute-start(f32[64,128]{1,0:T(8,128)S(1)} %merge.2.refs_0_), channel_id=1, source_target_pairs={{0,4},{1,5},{2,6},{3,7},{4,0},{5,1},{6,2},{7,3},{8,12},{9,13},{10,... | collective-permute-start | bytes 98312 | tf_op jit(solution)/shard_map/ppermute | solution.py:390
  24.2 0.5 collective-permute-start.1
  24.8 0.0 collective-permute-done.4.other_ref
  24.8 1.1 %couple.2 = f32[384,128]{1,0:T(8,128)} custom-call(f32[384,128]{1,0:T(8,128)S(1)} %bitcast.22, f32[384,128]{1,0:T(8,128)S(1)} %collective-permute-done.4.other_ref), custom_call_target="tpu_custom_call" | custom-call | flops 3200000 | bytes 600000 | tf_op jit(solution)/shard_map/couple/pallas_call | solution.py:319
  25.9 4.3 %all-to-all-start.1 = ((f32[16,24,128]{2,1,0:T(8,128)}), f32[16,24,128]{2,1,0:T(8,128)S(1)}, u32[]{:S(2)}, u32[]{:S(2)}) async-start(f32[16,24,128]{2,1,0:T(8,128)} %bitcast.9), calls=%async_computation.1 | async-start | bytes 393216 | tf_op jit(solution)/shard_map/all_to_all | solution.py:387
  30.2 0.0 collective-permute-done.3.refs_3_
  30.2 0.0 collective-permute-done.2.refs_2_
  30.2 0.0 collective-permute-done.1.refs_1_
  30.2 0.0 copy-done.4
  30.3 0.0 copy-done.5
  30.3 0.0 copy-done.6
  30.3 0.0 copy-done.7
  30.3 0.0 copy-start
  30.3 0.0 copy-start.1
  30.3 0.0 copy-start.3
  30.3 3.7 %flux_part.2 = (f32[384,128]{1,0:T(8,128)S(1)}, f32[384,128]{1,0:T(8,128)S(1)}) custom-call(s32[1]{0:T(128)S(6)} %copy.13.refs_2_.counts_hbm, s32[4]{0:T(128)S(1)} %bitcast.32, s32[4]{0:T(128)S(1)} %bitcast.34, f32[384,128]{1,0:T(8,128)} %bitcast.2.psi_hbm, s32[384,128]{1,0:T(8,128)S(1)} %bitcast.28, f32[384,128]{1,0:T(8,128)S(1)} %bitcast.30, ...), custom_call_target="tpu_custom_call" | custom-call | flops 30000001024 | bytes 7000000 | tf_op jit(solution)/shard_map/flux_part/pallas_call | solution.py:268
  34.0 0.0 copy-done
  34.0 0.0 copy-done.1
  34.0 0.9 %prepare.1 = (f32[2592,128]{1,0:T(8,128)S(1)}, f32[64,128]{1,0:T(8,128)S(1)}, f32[64,128]{1,0:T(8,128)S(1)}) custom-call(s32[1]{0:T(128)S(6)} %copy.13.refs_2_.counts_hbm, bf16[6,6,8192]{2,1,0:T(8,128)(2,1)S(1)} %bitcast.20, f32[64,128]{1,0:T(8,128)S(1)} %bitcast.25, f32[384,128]{1,0:T(8,128)S(1)} %get-tuple-element.22.after_ref.residual_ref), custom_call_target="tpu_custom_call" | custom-call | flops 1000000 | bytes 2500000 | tf_op jit(solution)/shard_map/prepare/pallas_call | solution.py:157
  35.0 4.2 %all-to-all-done.1 = f32[16,24,128]{2,1,0:T(8,128)S(1)} async-done(((f32[16,24,128]{2,1,0:T(8,128)}), f32[16,24,128]{2,1,0:T(8,128)S(1)}, u32[]{:S(2)}, u32[]{:S(2)}) %all-to-all-start.1) | async-done | bytes 196640 | tf_op jit(solution)/shard_map/all_to_all | solution.py:387
  39.1 0.0 copy-done.3
  39.1 0.9 %finish.2 = (f32[384,128]{1,0:T(8,128)}, f32[32,128]{1,0:T(8,128)S(1)}) custom-call(f32[384,128]{1,0:T(8,128)S(1)} %get-tuple-element.21.base_ref, f32[384,128]{1,0:T(8,128)S(1)} %get-tuple-element.22.after_ref.residual_ref, f32[384,128]{1,0:T(8,128)S(1)} %bitcast.18, f32[64,128]{1,0:T(8,128)S(1)} %get-tuple-element.24.live_ref, ...), custom_call_target="tpu_custom_call" | custom-call | flops 600000 | bytes 2000000 | tf_op jit(solution)/shard_map/finish/pallas_call | solution.py:368
  40.1 4.1 %all-to-all-start.2 = ((f32[16,24,128]{2,1,0:T(8,128)}), f32[16,24,128]{2,1,0:T(8,128)S(1)}, u32[]{:S(2)}, u32[]{:S(2)}) async-start(f32[16,24,128]{2,1,0:T(8,128)} %bitcast.13), calls=%async_computation.2 | async-start | bytes 393216 | tf_op jit(solution)/shard_map/all_to_all | solution.py:387
  44.1 3.1 %collective-permute-start.5 = (f32[32,128]{1,0:T(8,128)S(1)}, f32[32,128]{1,0:T(8,128)S(1)}, u32[]{:S(2)}, u32[]{:S(2)}) collective-permute-start(f32[32,128]{1,0:T(8,128)S(1)} %get-tuple-element.28.refs_0_), channel_id=1, source_target_pairs={{0,1},{1,0},{2,3},{3,2},{4,5},{5,4},{6,7},{7,6},{8,9},{9,8},{10,11... | collective-permute-start | bytes 49160 | tf_op jit(solution)/shard_map/ppermute | solution.py:390
  47.3 2.1 %collective-permute-done.5.refs_1_ = f32[32,128]{1,0:T(8,128)S(1)} collective-permute-done((f32[32,128]{1,0:T(8,128)S(1)}, f32[32,128]{1,0:T(8,128)S(1)}, u32[]{:S(2)}, u32[]{:S(2)}) %collective-permute-start.5) | collective-permute-done | bytes 16416 | tf_op jit(solution)/shard_map/ppermute | solution.py:390
  49.4 3.2 %all-to-all-done.2 = f32[16,24,128]{2,1,0:T(8,128)S(1)} async-done(((f32[16,24,128]{2,1,0:T(8,128)}), f32[16,24,128]{2,1,0:T(8,128)S(1)}, u32[]{:S(2)}, u32[]{:S(2)}) %all-to-all-start.2) | async-done | bytes 196640 | tf_op jit(solution)/shard_map/all_to_all | solution.py:387
  52.6 0.0 collective-permute-start.9
  52.6 2.8 %collective-permute-start.8 = (f32[64,128]{1,0:T(8,128)S(1)}, f32[64,128]{1,0:T(8,128)S(1)}, u32[]{:S(2)}, u32[]{:S(2)}) collective-permute-start(f32[64,128]{1,0:T(8,128)S(1)} %merge.3.refs_0_), channel_id=1, source_target_pairs={{0,6},{1,7},{2,4},{3,5},{4,2},{5,3},{6,0},{7,1},{8,14},{9,15},{10,... | collective-permute-start | bytes 98312 | tf_op jit(solution)/shard_map/ppermute | solution.py:390
  55.4 0.8 %collective-permute-start.7 = (f32[64,128]{1,0:T(8,128)S(1)}, f32[64,128]{1,0:T(8,128)S(1)}, u32[]{:S(2)}, u32[]{:S(2)}) collective-permute-start(f32[64,128]{1,0:T(8,128)S(1)} %merge.3.refs_0_), channel_id=1, source_target_pairs={{0,4},{1,5},{2,6},{3,7},{4,0},{5,1},{6,2},{7,3},{8,12},{9,13},{10,... | collective-permute-start | bytes 98312 | tf_op jit(solution)/shard_map/ppermute | solution.py:390
  56.2 0.5 collective-permute-start.6
  56.7 0.0 collective-permute-done.9.other_ref
  56.7 1.1 %couple.3 = f32[384,128]{1,0:T(8,128)} custom-call(f32[384,128]{1,0:T(8,128)S(1)} %bitcast.24, f32[384,128]{1,0:T(8,128)S(1)} %collective-permute-done.9.other_ref), custom_call_target="tpu_custom_call" | custom-call | flops 3200000 | bytes 600000 | tf_op jit(solution)/shard_map/couple/pallas_call | solution.py:319
  57.8 5.1 %all-to-all-start.3 = ((f32[16,24,128]{2,1,0:T(8,128)}), f32[16,24,128]{2,1,0:T(8,128)S(1)}, u32[]{:S(2)}, u32[]{:S(2)}) async-start(f32[16,24,128]{2,1,0:T(8,128)} %bitcast.15), calls=%async_computation.3 | async-start | bytes 393216 | tf_op jit(solution)/shard_map/all_to_all | solution.py:387
  62.9 0.0 collective-permute-done.8.refs_3_
  62.9 0.0 collective-permute-done.7.refs_2_
  63.0 0.0 collective-permute-done.6.refs_1_
  63.0 3.7 %flux_part.3 = (f32[384,128]{1,0:T(8,128)S(1)}, f32[384,128]{1,0:T(8,128)S(1)}) custom-call(s32[1]{0:T(128)S(6)} %copy.13.refs_2_.counts_hbm, s32[4]{0:T(128)S(1)} %bitcast.33, s32[4]{0:T(128)S(1)} %bitcast.35, f32[384,128]{1,0:T(8,128)} %get-tuple-element.27.psi_hbm, s32[384,128]{1,0:T(8,128)S(1)} %bitcast.29, f32[384,128]{1,0:T(8,128)S(1)} %bitcast.31, ...), custom_call_target="tpu_custom_call" | custom-call | flops 30000001024 | bytes 7000000 | tf_op jit(solution)/shard_map/flux_part/pallas_call | solution.py:268
  66.6 5.2 %all-to-all-done.3 = f32[16,24,128]{2,1,0:T(8,128)S(1)} async-done(((f32[16,24,128]{2,1,0:T(8,128)}), f32[16,24,128]{2,1,0:T(8,128)S(1)}, u32[]{:S(2)}, u32[]{:S(2)}) %all-to-all-start.3) | async-done | bytes 196640 | tf_op jit(solution)/shard_map/all_to_all | solution.py:387
  71.9 0.9 %finish.3 = f32[384,128]{1,0:T(8,128)} custom-call(f32[384,128]{1,0:T(8,128)S(1)} %get-tuple-element.30.base_ref, f32[384,128]{1,0:T(8,128)S(1)} %get-tuple-element.31.residual_ref, f32[384,128]{1,0:T(8,128)S(1)} %bitcast.19, f32[64,128]{1,0:T(8,128)S(1)} %get-tuple-element.24.live_ref, f32[64,128]{1,0:T(8,128)S(1)} %get-tuple-element.25.scale_ref, ...), custom_call_target="tpu_custom_call" | custom-call | flops 600000 | bytes 2000000 | tf_op jit(solution)/shard_map/finish/pallas_call | solution.py:368
  (2 shorter events, 0.0 us)
Async XLA Ops:
  0.0 0.7 copy-start.2
  0.7 29.6 %copy-start.4 = (s32[1,6,8192]{2,0,1:T(1,128)S(1)}, s32[1,6,8192]{2,0,1:T(1,128)}, u32[]{:S(2)}) copy-start(s32[1,6,8192]{2,0,1:T(1,128)} %param.16) | copy-start | bytes 589828
  0.7 29.6 %copy-start.5 = (f32[1,1,6,8192]{3,1,2,0:T(1,128)S(1)}, f32[1,1,6,8192]{3,1,2,0:T(1,128)}, u32[]{:S(2)}) copy-start(f32[1,1,6,8192]{3,1,2,0:T(1,128)} %param.11) | copy-start | bytes 589828
  0.7 29.6 %copy-start.6 = (s32[1,1,4]{2,1,0:T(1,128)S(1)}, s32[1,1,4]{2,1,0:T(1,128)}, u32[]{:S(2)}) copy-start(s32[1,1,4]{2,1,0:T(1,128)} %param.18) | copy-start | bytes 52
  0.7 29.6 %copy-start.7 = (s32[1,1,4]{2,1,0:T(1,128)S(1)}, s32[1,1,4]{2,1,0:T(1,128)}, u32[]{:S(2)}) copy-start(s32[1,1,4]{2,1,0:T(1,128)} %param.19) | copy-start | bytes 52
  1.9 18.8 %all-to-all-start = ((f32[16,24,128]{2,1,0:T(8,128)}), f32[16,24,128]{2,1,0:T(8,128)S(1)}, u32[]{:S(2)}, u32[]{:S(2)}) async-start(f32[16,24,128]{2,1,0:T(8,128)} %bitcast.7), calls=%async_computation | async-start | bytes 393216 | tf_op jit(solution)/shard_map/all_to_all | solution.py:387
  11.5 5.4 %collective-permute-start = (f32[32,128]{1,0:T(8,128)S(1)}, f32[32,128]{1,0:T(8,128)S(1)}, u32[]{:S(2)}, u32[]{:S(2)}) collective-permute-start(f32[32,128]{1,0:T(8,128)S(1)} %pack_donors.1.refs_0_), channel_id=1, source_target_pairs={{0,1},{1,0},{2,3},{3,2},{4,5},{5,4},{6,7},{7,6},{8,9},{9,8},{10,11... | collective-permute-start | bytes 49160 | tf_op jit(solution)/shard_map/ppermute | solution.py:390
  20.7 4.1 %collective-permute-start.4 = (f32[384,128]{1,0:T(8,128)S(1)}, f32[384,128]{1,0:T(8,128)S(1)}, u32[]{:S(2)}, u32[]{:S(2)}) collective-permute-start(f32[384,128]{1,0:T(8,128)S(1)} %bitcast.21), channel_id=1, source_target_pairs={{0,8},{8,0},{16,24},{24,16},{32,40},{40,32},{48,56},{56,48},{64,72... | collective-permute-start | bytes 589832 | tf_op jit(solution)/shard_map/ppermute | solution.py:405
  20.7 9.5 %collective-permute-start.3 = (f32[64,128]{1,0:T(8,128)S(1)}, f32[64,128]{1,0:T(8,128)S(1)}, u32[]{:S(2)}, u32[]{:S(2)}) collective-permute-start(f32[64,128]{1,0:T(8,128)S(1)} %merge.2.refs_0_), channel_id=1, source_target_pairs={{0,6},{1,7},{2,4},{3,5},{4,2},{5,3},{6,0},{7,1},{8,14},{9,15},{10,... | collective-permute-start | bytes 98312 | tf_op jit(solution)/shard_map/ppermute | solution.py:390
  23.4 6.8 %collective-permute-start.2 = (f32[64,128]{1,0:T(8,128)S(1)}, f32[64,128]{1,0:T(8,128)S(1)}, u32[]{:S(2)}, u32[]{:S(2)}) collective-permute-start(f32[64,128]{1,0:T(8,128)S(1)} %merge.2.refs_0_), channel_id=1, source_target_pairs={{0,4},{1,5},{2,6},{3,7},{4,0},{5,1},{6,2},{7,3},{8,12},{9,13},{10,... | collective-permute-start | bytes 98312 | tf_op jit(solution)/shard_map/ppermute | solution.py:390
  24.2 6.0 %collective-permute-start.1 = (f32[64,128]{1,0:T(8,128)S(1)}, f32[64,128]{1,0:T(8,128)S(1)}, u32[]{:S(2)}, u32[]{:S(2)}) collective-permute-start(f32[64,128]{1,0:T(8,128)S(1)} %merge.2.refs_0_), channel_id=1, source_target_pairs={{0,2},{1,3},{2,0},{3,1},{4,6},{5,7},{6,4},{7,5},{8,10},{9,11},{10,... | collective-permute-start | bytes 98312 | tf_op jit(solution)/shard_map/ppermute | solution.py:390
  25.9 13.3 %all-to-all-start.1 = ((f32[16,24,128]{2,1,0:T(8,128)}), f32[16,24,128]{2,1,0:T(8,128)S(1)}, u32[]{:S(2)}, u32[]{:S(2)}) async-start(f32[16,24,128]{2,1,0:T(8,128)} %bitcast.9), calls=%async_computation.1 | async-start | bytes 393216 | tf_op jit(solution)/shard_map/all_to_all | solution.py:387
  30.3 3.7 %copy-start = (bf16[1,1,6,6,8192]{4,3,2,1,0:T(8,128)(2,1)S(1)}, bf16[1,1,6,6,8192]{4,3,2,1,0:T(8,128)(2,1)}, u32[]{:S(2)}) copy-start(bf16[1,1,6,6,8192]{4,3,2,1,0:T(8,128)(2,1)} %param.13) | copy-start | bytes 1769476
  30.3 3.7 %copy-start.1 = (f32[1,8192]{1,0:T(1,128)S(1)}, f32[1,8192]{1,0:T(1,128)}, u32[]{:S(2)}) copy-start(f32[1,8192]{1,0:T(1,128)} %param.14) | copy-start | bytes 98308
  30.3 8.8 %copy-start.3 = (s32[1,512]{1,0:T(1,128)S(1)}, s32[1,512]{1,0:T(1,128)}, u32[]{:S(2)}) copy-start(s32[1,512]{1,0:T(1,128)} %param.17) | copy-start | bytes 6148
  40.1 12.6 %all-to-all-start.2 = ((f32[16,24,128]{2,1,0:T(8,128)}), f32[16,24,128]{2,1,0:T(8,128)S(1)}, u32[]{:S(2)}, u32[]{:S(2)}) async-start(f32[16,24,128]{2,1,0:T(8,128)} %bitcast.13), calls=%async_computation.2 | async-start | bytes 393216 | tf_op jit(solution)/shard_map/all_to_all | solution.py:387
  44.1 5.3 %collective-permute-start.5 = (f32[32,128]{1,0:T(8,128)S(1)}, f32[32,128]{1,0:T(8,128)S(1)}, u32[]{:S(2)}, u32[]{:S(2)}) collective-permute-start(f32[32,128]{1,0:T(8,128)S(1)} %get-tuple-element.28.refs_0_), channel_id=1, source_target_pairs={{0,1},{1,0},{2,3},{3,2},{4,5},{5,4},{6,7},{7,6},{8,9},{9,8},{10,11... | collective-permute-start | bytes 49160 | tf_op jit(solution)/shard_map/ppermute | solution.py:390
  52.6 4.1 %collective-permute-start.9 = (f32[384,128]{1,0:T(8,128)S(1)}, f32[384,128]{1,0:T(8,128)S(1)}, u32[]{:S(2)}, u32[]{:S(2)}) collective-permute-start(f32[384,128]{1,0:T(8,128)S(1)} %bitcast.23), channel_id=1, source_target_pairs={{0,8},{8,0},{16,24},{24,16},{32,40},{40,32},{48,56},{56,48},{64,72... | collective-permute-start | bytes 589832 | tf_op jit(solution)/shard_map/ppermute | solution.py:405
  52.6 10.3 %collective-permute-start.8 = (f32[64,128]{1,0:T(8,128)S(1)}, f32[64,128]{1,0:T(8,128)S(1)}, u32[]{:S(2)}, u32[]{:S(2)}) collective-permute-start(f32[64,128]{1,0:T(8,128)S(1)} %merge.3.refs_0_), channel_id=1, source_target_pairs={{0,6},{1,7},{2,4},{3,5},{4,2},{5,3},{6,0},{7,1},{8,14},{9,15},{10,... | collective-permute-start | bytes 98312 | tf_op jit(solution)/shard_map/ppermute | solution.py:390
  55.4 7.6 %collective-permute-start.7 = (f32[64,128]{1,0:T(8,128)S(1)}, f32[64,128]{1,0:T(8,128)S(1)}, u32[]{:S(2)}, u32[]{:S(2)}) collective-permute-start(f32[64,128]{1,0:T(8,128)S(1)} %merge.3.refs_0_), channel_id=1, source_target_pairs={{0,4},{1,5},{2,6},{3,7},{4,0},{5,1},{6,2},{7,3},{8,12},{9,13},{10,... | collective-permute-start | bytes 98312 | tf_op jit(solution)/shard_map/ppermute | solution.py:390
  56.2 6.8 %collective-permute-start.6 = (f32[64,128]{1,0:T(8,128)S(1)}, f32[64,128]{1,0:T(8,128)S(1)}, u32[]{:S(2)}, u32[]{:S(2)}) collective-permute-start(f32[64,128]{1,0:T(8,128)S(1)} %merge.3.refs_0_), channel_id=1, source_target_pairs={{0,2},{1,3},{2,0},{3,1},{4,6},{5,7},{6,4},{7,5},{8,10},{9,11},{10,... | collective-permute-start | bytes 98312 | tf_op jit(solution)/shard_map/ppermute | solution.py:390
  57.8 14.1 %all-to-all-start.3 = ((f32[16,24,128]{2,1,0:T(8,128)}), f32[16,24,128]{2,1,0:T(8,128)S(1)}, u32[]{:S(2)}, u32[]{:S(2)}) async-start(f32[16,24,128]{2,1,0:T(8,128)} %bitcast.15), calls=%async_computation.3 | async-start | bytes 393216 | tf_op jit(solution)/shard_map/all_to_all | solution.py:387
